TPU v7x, 32 devices: a whole 2x2x4 slice. The times are simulated.
32 devices in a mesh: gx: 8 (over z, y), gy: 4 (over x, core).
Axes of the slice: x: 2, y: 2, z: 4, core: 2. Of those that a mesh axis runs over, the one named last changes fastest.
Arguments:
- latents: bfloat16 [8, 4, 512, 128], P('gx', 'gy'), may hold values from -6 to 6
- edge_latents: bfloat16 [8, 4, 4096, 128], P('gx', 'gy'), may hold values from -6 to 6
- senders: int32 [8, 4, 4096], P('gx', 'gy'), may hold values from 0 to 1663, as said below
- receivers: int32 [8, 4, 4096], P('gx', 'gy'), may hold values from 0 to 255
- ghost_rows: int32 [8, 4, 3, 3, 128], P('gx', 'gy'), may hold values from 0 to 511
- edge_count: int32 [8, 4], P('gx', 'gy'), may hold values from 1024 to 4096, as said below
- node_cotangent: bfloat16 [8, 4, 512, 128], P('gx', 'gy'), may hold values from -6 to 6
- edge_cotangent: bfloat16 [8, 4, 4096, 128], P('gx', 'gy'), may hold values from -6 to 6
- edge_first: bfloat16 [2, 384, 128], replicated, may hold values from -0.3125 to 0.3125
- edge_second: bfloat16 [2, 128, 128], replicated, may hold values from -0.5 to 0.5
- edge_scale: float32 [2, 128], replicated, may hold values from 0.5 to 1.5
- node_first: bfloat16 [2, 256, 128], replicated, may hold values from -0.375 to 0.375
- node_second: bfloat16 [2, 128, 128], replicated, may hold values from -0.5 to 0.5
- node_scale: float32 [2, 128], replicated, may hold values from 0.5 to 1.5
Outputs:
- nodes_out: bfloat16 [8, 4, 512, 128], P('gx', 'gy')
- edges_out: bfloat16 [8, 4, 4096, 128], P('gx', 'gy')
- latents_grad: float32 [8, 4, 512, 128], P('gx', 'gy')
- edge_latents_grad: float32 [8, 4, 4096, 128], P('gx', 'gy')
- edge_first_grad: float32 [2, 384, 128], replicated
- edge_second_grad: float32 [2, 128, 128], replicated
- edge_scale_grad: float32 [2, 128], replicated
- node_first_grad: float32 [2, 256, 128], replicated
- node_second_grad: float32 [2, 128, 128], replicated
- node_scale_grad: float32 [2, 128], replicated
Inputs may be any that keep to these rules, and one draw needn't show every extreme that they name: `senders`: rows 0 to 511 of the node table are the domain's particles; row 512 + k * 128 + j is ghost row j of slot k = 3 a + b, from the neighbour at offset (a - 1, b - 1); slot 4 is never named. `edge_count`: edge slots at positions below the count are live, later ones are padding.
All inputs are finite; a program needn't handle non-finite values.
Results may differ from a plain program's by a relative error of at most 0.02.
Values may be sent and summed in bfloat16 or wider, within the bound.
A program may use at most 128 MiB of HBM per device.

v0:
```python
import functools

import jax
import jax.numpy as jnp
from jax import lax
from jax.experimental import pallas as pl
from jax.experimental.pallas import tpu as pltpu
from jax.sharding import PartitionSpec as P

L = 128
LAYERS = 2
TILE = 256
DEG = 8
SPAN = TILE * DEG
EPS = 1e-05
MESH = pl.DeviceIdType.MESH
F32 = jnp.float32
BF = jnp.bfloat16
VMEM = pl.BlockSpec(memory_space=pltpu.VMEM)
SMEM = pl.BlockSpec(memory_space=pltpu.SMEM)
OFFSETS = [(a - 1, b - 1) for a in range(3) for b in range(3) if (a, b) != (1, 1)]
SLOTS = len(OFFSETS)


def mm(a, b):
    return jnp.dot(a, b, preferred_element_type=F32)


def mm_nt(a, b):
    return lax.dot_general(a, b, (((1,), (1,)), ((), ())), preferred_element_type=F32)


def mm_tn(a, b):
    return lax.dot_general(a, b, (((0,), (0,)), ((), ())), preferred_element_type=F32)


def hot(mask):
    return jnp.where(mask, 1.0, 0.0).astype(BF)


def down(ids_row, width=L):
    n = ids_row.shape[1]
    return jnp.broadcast_to(ids_row, (L, n)).T


def picks(column, size):
    lane = lax.broadcasted_iota(jnp.int32, column.shape, 1)
    return jnp.concatenate([hot(column == lane + k) for k in range(0, size, L)], axis=1)


def drops(ids_row, first, size):
    row = lax.broadcasted_iota(jnp.int32, (size, ids_row.shape[1]), 0)
    return hot(row + first == ids_row)


def silu(v):
    return v / (1.0 + jnp.exp(-v))


def silu_slope(v):
    s = 1.0 / (1.0 + jnp.exp(-v))
    return s * (1.0 + v * (1.0 - s))


def standard(v):
    center = jnp.mean(v, axis=-1, keepdims=True)
    off = v - center
    inv = lax.rsqrt(jnp.mean(off * off, axis=-1, keepdims=True) + EPS)
    return off * inv, inv


def standard_back(g, hat, inv):
    a = jnp.mean(g, axis=-1, keepdims=True)
    b = jnp.mean(g * hat, axis=-1, keepdims=True)
    return inv * (g - a - hat * b)


def live(count, b):
    row = lax.broadcasted_iota(jnp.int32, (TILE, L), 0) + b * TILE
    return jnp.where(row < count, 1.0, 0.0)


def rows_of(b):
    return pl.ds(pl.multiple_of(b * TILE, TILE), TILE)


def forward(nodes, ghosts, edges, send, recv, count, w, table, msg, pre_out, edges_out,
            inb_out, nodes_out):
    ef, es, esc, nf, ns, nsc = w
    p = nodes.shape[0]
    size = p + ghosts.shape[0]
    blocks = edges.shape[0] // TILE
    ws, wr, we = (ef[i * L:(i + 1) * L, :] for i in range(3))
    table[:p, :] = mm(nodes[...], ws).astype(BF)
    table[p:size, :] = mm(ghosts[...], ws).astype(BF)
    table[size:size + p, :] = mm(nodes[...], wr).astype(BF)

    def block(b, carry):
        rows = rows_of(b)
        tile = pl.ds(pl.multiple_of(size + (b // DEG) * TILE, TILE), TILE)
        pre = (
            mm(picks(down(send[pl.ds(b, 1), :]), size), table[:size, :])
            + mm(picks(down(recv[pl.ds(b, 1), :]), TILE), table[tile, :])
            + mm(edges[rows, :], we)
        )
        pre_out[rows, :] = pre
        hat, _ = standard(mm(silu(pre).astype(BF), es[...]))
        message = hat * esc[...] * live(count, b)
        edges_out[rows, :] = (edges[rows, :].astype(F32) + message).astype(BF)
        msg[rows, :] = message.astype(BF)
        return carry

    lax.fori_loop(0, blocks, block, 0, unroll=2)
    for t in range(p // TILE):
        total = jnp.zeros((TILE, L), F32)
        for j in range(DEG):
            b = t * DEG + j
            total += mm(drops(recv[b:b + 1, :], 0, TILE), msg[b * TILE:(b + 1) * TILE, :])
        inb_out[t * TILE:(t + 1) * TILE, :] = total.astype(BF)
    pre_n = mm(nodes[...], nf[:L, :]) + mm(inb_out[...], nf[L:, :])
    hat, _ = standard(mm(silu(pre_n).astype(BF), ns[...]))
    nodes_out[...] = (nodes[...].astype(F32) + hat * nsc[...]).astype(BF)


def backward(nodes, ghosts, edges, send, send_flat, recv, count, w, pre_in, inb, node_ct, edge_ct,
             hid, du, dpre, edge_grad, ghost_grad, grads):
    ef, es, esc, nf, ns, nsc = w
    p = nodes.shape[0]
    ghost_n = ghosts.shape[0]
    blocks = edges.shape[0] // TILE
    ws, wr, we = (ef[i * L:(i + 1) * L, :] for i in range(3))
    nb = nodes[...]
    pre_n = mm(nb, nf[:L, :]) + mm(inb[...], nf[L:, :])
    hid_n = silu(pre_n).astype(BF)
    hat, inv = standard(mm(hid_n, ns[...]))
    node_scale_grad = jnp.sum(node_ct * hat, axis=0, keepdims=True)
    du_n = standard_back(node_ct * nsc[...], hat, inv).astype(BF)
    dpre_n = (mm_nt(du_n, ns[...]).astype(BF).astype(F32) * silu_slope(pre_n)).astype(BF)
    grads[512:640, :] = mm_tn(nb, dpre_n)
    grads[640:768, :] = mm_tn(inb[...], dpre_n)
    grads[768:896, :] = mm_tn(hid_n, du_n)
    node_grad = node_ct + mm_nt(dpre_n, nf[:L, :])
    dinb = mm_nt(dpre_n, nf[L:, :]).astype(BF)
    tiles = [dinb[t * TILE:(t + 1) * TILE, :] for t in range(p // TILE)]

    def block(tile_grad):
        def body(b, scale_grad):
            rows = rows_of(b)
            pre = pre_in[rows, :]
            h = silu(pre).astype(BF)
            hat, inv = standard(mm(h, es[...]))
            ect = edge_ct[rows, :].astype(F32)
            dm = (ect + mm(picks(down(recv[pl.ds(b, 1), :]), TILE), tile_grad)) * live(count, b)
            scale_grad = scale_grad + jnp.sum(dm * hat, axis=0, keepdims=True)
            d = standard_back(dm * esc[...], hat, inv).astype(BF)
            dp = (mm_nt(d, es[...]) * silu_slope(pre)).astype(BF)
            hid[rows, :] = h
            du[rows, :] = d
            dpre[rows, :] = dp
            edge_grad[rows, :] = (ect + mm_nt(dp, we)).astype(edge_grad.dtype)
            return scale_grad
        return body

    scale_grad = jnp.zeros((1, L), F32)
    for t, tile_grad in enumerate(tiles):
        scale_grad = lax.fori_loop(t * DEG, (t + 1) * DEG, block(tile_grad), scale_grad, unroll=2)
    grads[384:512, :] = mm_tn(hid[...], du[...])
    grads[256:384, :] = mm_tn(edges[...], dpre[...])
    row = lax.broadcasted_iota(jnp.int32, (16, L), 0)
    grads[896:912, :] = jnp.where(row == 0, scale_grad, jnp.where(row == 1, node_scale_grad, 0.0))
    parts = []
    for t in range(p // TILE):
        total = jnp.zeros((TILE, L), F32)
        for j in range(DEG):
            b = t * DEG + j
            total += mm(drops(recv[b:b + 1, :], 0, TILE), dpre[b * TILE:(b + 1) * TILE, :])
        parts.append(total.astype(BF))
    gr = jnp.concatenate(parts, axis=0)
    grads[L:2 * L, :] = mm_tn(nb, gr)
    node_grad = node_grad + mm_nt(gr, wr)
    ids = send_flat[...]
    parts = [
        mm(drops(ids, k, L), dpre[...]).astype(BF) for k in range(0, p + ghost_n, L)
    ]
    gs = jnp.concatenate(parts[:p // L], axis=0)
    gg = jnp.concatenate(parts[p // L:], axis=0)
    grads[:L, :] = mm_tn(nb, gs) + mm_tn(ghosts[...], gg)
    ghost_grad[...] = mm_nt(gg, ws).astype(BF)
    return node_grad + mm_nt(gs, ws)


def pick_ghosts(nodes, ghost_ids, picked):
    for c in range(SLOTS):
        picked[c * L:(c + 1) * L, :] = mm(
            picks(down(ghost_ids[c:c + 1, :]), nodes.shape[0]), nodes[...]
        ).astype(BF)


def put_back(ghost_flat, returned, p):
    return jnp.concatenate(
        [mm(drops(ghost_flat[...], k, L), returned[...]) for k in range(0, p, L)], axis=0
    )


def pick_kernel(nodes, ghost_ids, picked):
    pick_ghosts(nodes, ghost_ids, picked)


def first_kernel(count, nodes, ghosts, edges, send, recv, ghost_ids, ef, es, esc, nf, ns, nsc,
                 pre, edges_out, inb, nodes_out, picked, table, msg):
    forward(nodes, ghosts, edges, send, recv, count[0], (ef, es, esc, nf, ns, nsc), table, msg,
            pre, edges_out, inb, nodes_out)
    pick_ghosts(nodes_out, ghost_ids, picked)


def last_kernel(count, nodes, ghosts, edges, send, send_flat, recv, node_ct, edge_ct, ef, es, esc,
                nf, ns, nsc, edges_out, nodes_out, edge_grad, ghost_grad, grads, node_grad,
                table, msg, pre, inb, hid, du, dpre):
    w = (ef, es, esc, nf, ns, nsc)
    forward(nodes, ghosts, edges, send, recv, count[0], w, table, msg, pre, edges_out, inb,
            nodes_out)
    node_grad[...] = backward(nodes, ghosts, edges, send, send_flat, recv, count[0], w, pre, inb,
                              node_ct[...].astype(F32), edge_ct, hid, du, dpre, edge_grad,
                              ghost_grad, grads)


def low_kernel(count, nodes, ghosts, edges, send, send_flat, recv, ghost_flat, upper_grad,
               returned, edge_ct, pre, inb, ef, es, esc, nf, ns, nsc,
               edge_grad, ghost_grad, grads, node_grad, hid, du, dpre):
    w = (ef, es, esc, nf, ns, nsc)
    ct = upper_grad[...] + put_back(ghost_flat, returned, nodes.shape[0])
    node_grad[...] = backward(nodes, ghosts, edges, send, send_flat, recv, count[0], w, pre, inb,
                              ct.astype(BF).astype(F32), edge_ct, hid, du, dpre, edge_grad,
                              ghost_grad, grads)


def neighbours(gx, gy):
    x, y = lax.axis_index("gx"), lax.axis_index("gy")
    found = []
    for dx, dy in OFFSETS:
        there = (x + dx >= 0) & (x + dx < gx) & (y + dy >= 0) & (y + dy < gy)
        found.append((there, (lax.rem(x + dx + gx, gx), lax.rem(y + dy + gy, gy))))
    return found


def swap(found, src, dst, send_sem, recv_sem):
    copies = [
        pltpu.make_async_remote_copy(
            src_ref=src.at[c],
            dst_ref=dst.at[SLOTS - 1 - c],
            send_sem=send_sem.at[c],
            recv_sem=recv_sem.at[SLOTS - 1 - c],
            device_id=place,
            device_id_type=MESH,
        )
        for c, (_, place) in enumerate(found)
    ]
    for (there, _), copy in zip(found, copies):
        pl.when(there)(copy.start)
    return copies


def finish_swap(found, copies, src, dst, send_sem, recv_sem):
    for c, ((there, place), copy) in enumerate(zip(found, copies)):
        pl.when(there)(copy.wait_send)
        arrival = pltpu.make_async_remote_copy(
            src_ref=src.at[c], dst_ref=dst.at[c], send_sem=send_sem.at[c],
            recv_sem=recv_sem.at[c], device_id=place, device_id_type=MESH,
        )
        pl.when(there)(arrival.wait_recv)


def swap_kernel(gx, gy, src, dst, send_sem, recv_sem):
    found = neighbours(gx, gy)
    barrier = pltpu.get_barrier_semaphore()
    for there, place in found:
        @pl.when(there)
        def _():
            pl.semaphore_signal(barrier, inc=1, device_id=place, device_id_type=MESH)
    for c, (there, _) in enumerate(found):
        @pl.when(jnp.logical_not(there))
        def _():
            dst[c] = jnp.zeros(dst.shape[1:], dst.dtype)
    peers = sum(jnp.where(there, 1, 0) for there, _ in found)
    pl.semaphore_wait(barrier, peers)
    copies = swap(found, src, dst, send_sem, recv_sem)
    finish_swap(found, copies, src, dst, send_sem, recv_sem)


def solution(mesh):
    gx, gy = mesh.shape["gx"], mesh.shape["gy"]

    def call(kernel, shapes, scratch, args, smem_first=True, **params):
        return pl.pallas_call(
            kernel,
            out_shape=shapes,
            in_specs=[SMEM if smem_first and i == 0 else VMEM for i in range(len(args))],
            out_specs=jax.tree.map(lambda _: VMEM, shapes),
            scratch_shapes=scratch,
            compiler_params=pltpu.CompilerParams(vmem_limit_bytes=48 * 2**20, **params),
        )(*args)

    def exchange(value, collective_id):
        shape = (SLOTS, value.shape[0] // SLOTS, L)
        out = call(
            functools.partial(swap_kernel, gx, gy),
            jax.ShapeDtypeStruct(shape, BF),
            [pltpu.SemaphoreType.DMA((SLOTS,)), pltpu.SemaphoreType.DMA((SLOTS,))],
            (value.reshape(shape),),
            smem_first=False,
            collective_id=collective_id,
            has_side_effects=True,
        )
        return out.reshape(value.shape)

    def on_device(latents, edge_latents, senders, receivers, ghost_rows, edge_count,
                  node_cotangent, edge_cotangent, edge_first, edge_second, edge_scale,
                  node_first, node_second, node_scale):
        nodes, edges = latents[0, 0], edge_latents[0, 0]
        p, e = nodes.shape[0], edges.shape[0]
        g = ghost_rows.shape[-1]
        ghost_n = SLOTS * g
        ids = senders[0, 0]
        ids = jnp.where(ids >= p + 4 * g, ids - g, ids)
        send, send_flat = ids.reshape(-1, TILE), ids.reshape(1, -1)
        recv = receivers[0, 0].reshape(-1, TILE)
        slots = ghost_rows[0, 0].reshape(9, g)
        ghost_ids = jnp.concatenate([slots[:4], slots[5:]], axis=0)
        ghost_flat = ghost_ids.reshape(1, -1)
        count = edge_count.reshape(1)
        weights = [
            (edge_first[i], edge_second[i], edge_scale[i:i + 1], node_first[i], node_second[i],
             node_scale[i:i + 1])
            for i in range(LAYERS)
        ]

        def s(shape, dtype):
            return jax.ShapeDtypeStruct(shape, dtype)

        back_scratch = [pltpu.VMEM((e, L), BF)] * 3
        fore_scratch = [pltpu.VMEM((2 * p + ghost_n, L), BF), pltpu.VMEM((e, L), BF)]
        grad_rows = s((912, L), F32)

        picked = call(pick_kernel, s((ghost_n, L), BF), [], (nodes, ghost_ids), smem_first=False)
        ghosts0 = exchange(picked, 0)
        pre0, edges1, inb0, nodes1, picked1 = call(
            first_kernel,
            (s((e, L), F32), s((e, L), BF), s((p, L), BF), s((p, L), BF), s((ghost_n, L), BF)),
            fore_scratch,
            (count, nodes, ghosts0, edges, send, recv, ghost_ids, *weights[0]),
        )
        ghosts1 = exchange(picked1, 1)
        edges_out, nodes_out, edge_ct, ghost_ct, grads1, upper = call(
            last_kernel,
            (s((e, L), BF), s((p, L), BF), s((e, L), BF), s((ghost_n, L), BF), grad_rows,
             s((p, L), F32)),
            fore_scratch + [pltpu.VMEM((e, L), F32), pltpu.VMEM((p, L), BF)] + back_scratch,
            (count, nodes1, ghosts1, edges1, send, send_flat, recv, node_cotangent[0, 0],
             edge_cotangent[0, 0], *weights[1]),
        )
        total1 = lax.psum(grads1, ("gx", "gy"))
        returned1 = exchange(ghost_ct, 2)
        edge_grad, ghost_ct0, grads0, lower = call(
            low_kernel,
            (s((e, L), F32), s((ghost_n, L), BF), grad_rows, s((p, L), F32)),
            back_scratch,
            (count, nodes, ghosts0, edges, send, send_flat, recv, ghost_flat, upper, returned1,
             edge_ct, pre0, inb0, *weights[0]),
        )
        total0 = lax.psum(grads0, ("gx", "gy"))
        returned0 = exchange(ghost_ct0, 3)

        def end_kernel(ids_ref, lower_ref, returned_ref, out):
            out[...] = lower_ref[...] + put_back(ids_ref, returned_ref, p)

        node_grad = call(end_kernel, s((p, L), F32), [], (ghost_flat, lower, returned0),
                         smem_first=False)
        totals = jnp.stack([total0, total1])
        return (
            nodes_out[None, None],
            edges_out[None, None],
            node_grad[None, None],
            edge_grad[None, None],
            totals[:, :384],
            totals[:, 384:512],
            totals[:, 896],
            totals[:, 512:768],
            totals[:, 768:896],
            totals[:, 897],
        )

    cell = P("gx", "gy", None, None)
    line = P("gx", "gy", None)
    return jax.shard_map(
        on_device,
        mesh=mesh,
        in_specs=(cell, cell, line, line, P("gx", "gy", None, None, None), P("gx", "gy"), cell,
                  cell) + (P(),) * 6,
        out_specs=(cell,) * 4 + (P(),) * 6,
        check_vma=False,
    )
```

profile of v0, /device:TPU:0, one launch (start us, length us, event | category | flops | bytes accessed | tf_op | source)
XLA Modules:
  0.0 237.2 jit_solution(3941755765204710158)
XLA Ops:
  8.0 0.7 reduce
  8.7 0.7 compare_select_fusion.send_flat
  9.9 1.4 reduce.7
  11.4 1.4 reduce.8
  12.8 0.9 slice_bitcast_fusion.2
  13.7 1.0 slice_bitcast_fusion
  14.7 0.9 copy-done.2
  16.1 7.2 %shard_map.214 = bf16[8,128,128]{2,1,0:T(8,128)(2,1)S(1)} custom-call(bf16[8,128,128]{2,1,0:T(8,128)(2,1)S(1)} %bitcast.54), custom_call_target="tpu_custom_call" | custom-call | tf_op jit(solution)/shard_map/pallas_call | solution.py:294
  23.2 0.8 fusion.3
  24.0 0.8 slice_bitcast_fusion.4
  24.8 0.9 copy-done.3
  25.7 11.3 %shard_map.215 = (f32[4096,128]{1,0:T(8,128)S(1)}, bf16[4096,128]{1,0:T(8,128)(2,1)S(1)}, bf16[512,128]{1,0:T(8,128)(2,1)S(1)}, bf16[512,128]{1,0:T(8,128)(2,1)S(1)}, bf16[1024,128]{1,0:T(8,128)(2,1)S(1)}) custom-call(s32[1]{0:T(128)} %bitcast.40.count, bf16[512,128]{1,0:T(8,128)(2,1)S(1)} %bitcast.48, bf16[1024,128]{1,0:T(8,128)(2,1)S(1)} %bitcast.45, ...), custom_call_target="tpu_custom_call" | custom-call | tf_op jit(solution)/shard_map/pallas_call | solution.py:294
  37.1 1.3 copy-done.1
  38.4 7.3 %shard_map.216 = bf16[8,128,128]{2,1,0:T(8,128)(2,1)S(1)} custom-call(bf16[8,128,128]{2,1,0:T(8,128)(2,1)S(1)} %bitcast.57), custom_call_target="tpu_custom_call" | custom-call | tf_op jit(solution)/shard_map/pallas_call | solution.py:294
  45.7 25.9 %shard_map.217 = (bf16[4096,128]{1,0:T(8,128)(2,1)}, bf16[512,128]{1,0:T(8,128)(2,1)}, bf16[4096,128]{1,0:T(8,128)(2,1)S(1)}, bf16[1024,128]{1,0:T(8,128)(2,1)S(...) custom-call(s32[1]{0:T(128)} %bitcast.41.count, bf16[512,128]{1,0:T(8,128)(2,1)S(1)} %get-tuple-element.25.nodes, ...), custom_call_target="tpu_custom_call" | custom-call | tf_op jit(solution)/shard_map/pallas_call | solution.py:294
  71.6 7.2 %shard_map.218 = bf16[8,128,128]{2,1,0:T(8,128)(2,1)S(1)} custom-call(bf16[8,128,128]{2,1,0:T(8,128)(2,1)S(1)} %bitcast.56), custom_call_target="tpu_custom_call" | custom-call | tf_op jit(solution)/shard_map/pallas_call | solution.py:294
  78.8 17.2 %shard_map.219 = (f32[4096,128]{1,0:T(8,128)}, bf16[1024,128]{1,0:T(8,128)(2,1)S(1)}, f32[912,128]{1,0:T(8,128)}, f32[512,128]{1,0:T(8,128)S(1)}) custom-call(s32[1]{0:T(128)} %bitcast.42.count, bf16[512,128]{1,0:T(8,128)(2,1)S(1)} %bitcast.49, bf16[1024,128]{1,0:T(8,128)(2,1)S(1)} %bitcast.46, bf16[4096,128]{1,0:T(8,128)(2,1)S(1)} %bitcast.44, ...), custom_call_target="tpu_custom_call" | custom-call | tf_op jit(solution)/shard_map/pallas_call | solution.py:294
  96.0 7.1 %shard_map.220 = bf16[8,128,128]{2,1,0:T(8,128)(2,1)S(1)} custom-call(bf16[8,128,128]{2,1,0:T(8,128)(2,1)S(1)} %bitcast.55), custom_call_target="tpu_custom_call" | custom-call | tf_op jit(solution)/shard_map/pallas_call | solution.py:294
  103.2 1.1 shard_map.221
  104.3 121.2 %all-reduce.3.cloned.1.call-done = (f32[1,912,128]{2,1,0:T(8,128)}, f32[1,912,128]{2,1,0:T(8,128)}) async-done(((f32[1,912,128]{2,1,0:T(8,128)}, f32[1,912,128]{2,1,0:T(8,128)}), (f32[1,912,128]{2,1,0:T(8,128)}, f32[1,912,128]{2,1,0:T(8,128)})) %all-reduce.3.cloned.1.call-update) | async-done | bytes 933904 | tf_op jit(solution)/shard_map/psum | solution.py:370
  225.5 1.1 constant_dynamic-update-slice_fusion.1
  226.6 1.1 constant_dynamic-update-slice_fusion
  228.2 0.7 slice.85
  229.6 0.8 slice.82
  (23 shorter events, 2.4 us)
Async XLA Ops:
  7.2 17.6 %copy-start = (bf16[1,1,4096,128]{3,2,1,0:T(8,128)(2,1)S(1)}, bf16[1,1,4096,128]{3,2,1,0:T(8,128)(2,1)}, u32[]{:S(2)}) copy-start(bf16[1,1,4096,128]{3,2,1,0:T(8,128)(2,1)} %param.15) | copy-start | bytes 3145732
  7.2 218.3 %all-reduce.3.cloned.1.call-start = ((), (), s32[]{:S(2)}) async-start(), calls=%async_computation | async-start | bytes 1867776 | tf_op jit(solution)/shard_map/psum | solution.py:370
  14.7 0.9 copy-start.2
  15.6 30.1 %copy-start.5 = (bf16[1,1,4096,128]{3,2,1,0:T(8,128)(2,1)S(1)}, bf16[1,1,4096,128]{3,2,1,0:T(8,128)(2,1)}, u32[]{:S(2)}) copy-start(bf16[1,1,4096,128]{3,2,1,0:T(8,128)(2,1)} %param.21) | copy-start | bytes 3145732
  24.8 0.9 copy-start.3
  25.7 19.9 %copy-start.6 = (bf16[1,1,512,128]{3,2,1,0:T(8,128)(2,1)S(1)}, bf16[1,1,512,128]{3,2,1,0:T(8,128)(2,1)}, u32[]{:S(2)}) copy-start(bf16[1,1,512,128]{3,2,1,0:T(8,128)(2,1)} %param.20) | copy-start | bytes 393220
  37.0 1.3 copy-start.1
  38.4 40.4 %copy-start.4 = (bf16[1,1,512,128]{3,2,1,0:T(8,128)(2,1)S(1)}, bf16[1,1,512,128]{3,2,1,0:T(8,128)(2,1)}, u32[]{:S(2)}) copy-start(bf16[1,1,512,128]{3,2,1,0:T(8,128)(2,1)} %param.14) | copy-start | bytes 393220
Sparse Core Ops, SparseCore 0:
  96.2 129.3 all-reduce.2
where the time goes:
time: 238 us; the launch traced here: 237 us
  waiting for transfers between devices  121 us (51%)
  Pallas kernels  84.8 us (36%)
  between operations  14.9 us (6%)
  local copies, waits for them, and re-layouts  12 us (5%)
  other arithmetic  4.27 us (2%)
    psum x1, waiting for transfers between devices, on_device(): total0 = lax.psum(grads0, ('gx', 'gy'))  121 us
    pallas_call x9, Pallas kernels, call(): pl.pallas_call(kernel, out_shape=shapes, in_specs=[SMEM if smem_first and...  84.8 us
  transfers between devices with their start and end apart: 1, of which 1 were waited for; matrix products, arithmetic and copies ran while one was open for 0% of the time, Pallas kernels for 3%

commit v1 on v0

--- a/solution.py
+++ b/solution.py
@@ -16,6 +16,7 @@
 MESH = pl.DeviceIdType.MESH
 F32 = jnp.float32
 BF = jnp.bfloat16
+I16 = jnp.int16
 VMEM = pl.BlockSpec(memory_space=pltpu.VMEM)
 SMEM = pl.BlockSpec(memory_space=pltpu.SMEM)
 OFFSETS = [(a - 1, b - 1) for a in range(3) for b in range(3) if (a, b) != (1, 1)]
@@ -35,22 +36,23 @@
 
 
 def hot(mask):
-    return jnp.where(mask, 1.0, 0.0).astype(BF)
+    return jnp.where(mask, jnp.ones((), BF), jnp.zeros((), BF))
 
 
 def down(ids_row, width=L):
     n = ids_row.shape[1]
-    return jnp.broadcast_to(ids_row, (L, n)).T
+    return jnp.broadcast_to(ids_row, (L, n)).T.astype(I16)
 
 
 def picks(column, size):
-    lane = lax.broadcasted_iota(jnp.int32, column.shape, 1)
-    return jnp.concatenate([hot(column == lane + k) for k in range(0, size, L)], axis=1)
+    lane = lax.broadcasted_iota(jnp.int32, column.shape, 1).astype(I16)
+    return jnp.concatenate([hot(column == lane + jnp.int16(k)) for k in range(0, size, L)], axis=1)
 
 
 def drops(ids_row, first, size):
-    row = lax.broadcasted_iota(jnp.int32, (size, ids_row.shape[1]), 0)
-    return hot(row + first == ids_row)
+    shape = (size, ids_row.shape[1])
+    row = lax.broadcasted_iota(jnp.int32, shape, 0) + first
+    return hot(row.astype(I16) == jnp.broadcast_to(ids_row, shape).astype(I16))
 
 
 def silu(v):
@@ -84,25 +86,37 @@
     return pl.ds(pl.multiple_of(b * TILE, TILE), TILE)
 
 
+def table_ids(ids, p, g):
+    return jnp.where(ids >= p + 4 * g, ids - g, ids)
+
+
+def ghost_row(ghost_ids, c):
+    a, b = divmod(c + (c >= 4), 3)
+    return ghost_ids[0, 0, a, b:b + 1, :]
+
+
 def forward(nodes, ghosts, edges, send, recv, count, w, table, msg, pre_out, edges_out,
             inb_out, nodes_out):
     ef, es, esc, nf, ns, nsc = w
     p = nodes.shape[0]
+    g = ghosts.shape[0] // SLOTS
     size = p + ghosts.shape[0]
-    blocks = edges.shape[0] // TILE
     ws, wr, we = (ef[i * L:(i + 1) * L, :] for i in range(3))
     table[:p, :] = mm(nodes[...], ws).astype(BF)
     table[p:size, :] = mm(ghosts[...], ws).astype(BF)
-    table[size:size + p, :] = mm(nodes[...], wr).astype(BF)
+    table[size + TILE:size + TILE + L, :] = we
 
     def block(b, carry):
         rows = rows_of(b)
-        tile = pl.ds(pl.multiple_of(size + (b // DEG) * TILE, TILE), TILE)
-        pre = (
-            mm(picks(down(send[pl.ds(b, 1), :]), size), table[:size, :])
-            + mm(picks(down(recv[pl.ds(b, 1), :]), TILE), table[tile, :])
-            + mm(edges[rows, :], we)
-        )
+        left = jnp.concatenate(
+            [
+                picks(down(table_ids(send[:, rows], p, g)), size),
+                picks(down(recv[:, rows]), TILE),
+                edges[rows, :],
+            ],
+            axis=1,
+        )
+        pre = mm(left, table[...])
         pre_out[rows, :] = pre
         hat, _ = standard(mm(silu(pre).astype(BF), es[...]))
         message = hat * esc[...] * live(count, b)
@@ -110,19 +124,22 @@
         msg[rows, :] = message.astype(BF)
         return carry
 
-    lax.fori_loop(0, blocks, block, 0, unroll=2)
+    for t in range(p // TILE):
+        table[size:size + TILE, :] = mm(nodes[t * TILE:(t + 1) * TILE, :], wr).astype(BF)
+        lax.fori_loop(t * DEG, (t + 1) * DEG, block, 0, unroll=4)
     for t in range(p // TILE):
         total = jnp.zeros((TILE, L), F32)
         for j in range(DEG):
             b = t * DEG + j
-            total += mm(drops(recv[b:b + 1, :], 0, TILE), msg[b * TILE:(b + 1) * TILE, :])
+            at = slice(b * TILE, (b + 1) * TILE)
+            total += mm(drops(recv[:, at], 0, TILE), msg[at, :])
         inb_out[t * TILE:(t + 1) * TILE, :] = total.astype(BF)
     pre_n = mm(nodes[...], nf[:L, :]) + mm(inb_out[...], nf[L:, :])
     hat, _ = standard(mm(silu(pre_n).astype(BF), ns[...]))
     nodes_out[...] = (nodes[...].astype(F32) + hat * nsc[...]).astype(BF)
 
 
-def backward(nodes, ghosts, edges, send, send_flat, recv, count, w, pre_in, inb, node_ct, edge_ct,
+def backward(nodes, ghosts, edges, send, recv, count, w, pre_in, inb, node_ct, edge_ct,
              hid, du, dpre, edge_grad, ghost_grad, grads):
     ef, es, esc, nf, ns, nsc = w
     p = nodes.shape[0]
@@ -136,9 +153,9 @@
     node_scale_grad = jnp.sum(node_ct * hat, axis=0, keepdims=True)
     du_n = standard_back(node_ct * nsc[...], hat, inv).astype(BF)
     dpre_n = (mm_nt(du_n, ns[...]).astype(BF).astype(F32) * silu_slope(pre_n)).astype(BF)
-    grads[512:640, :] = mm_tn(nb, dpre_n)
-    grads[640:768, :] = mm_tn(inb[...], dpre_n)
-    grads[768:896, :] = mm_tn(hid_n, du_n)
+    grads[512:640, :] = mm_tn(nb, dpre_n).astype(BF)
+    grads[640:768, :] = mm_tn(inb[...], dpre_n).astype(BF)
+    grads[768:896, :] = mm_tn(hid_n, du_n).astype(BF)
     node_grad = node_ct + mm_nt(dpre_n, nf[:L, :])
     dinb = mm_nt(dpre_n, nf[L:, :]).astype(BF)
     tiles = [dinb[t * TILE:(t + 1) * TILE, :] for t in range(p // TILE)]
@@ -150,7 +167,7 @@
             h = silu(pre).astype(BF)
             hat, inv = standard(mm(h, es[...]))
             ect = edge_ct[rows, :].astype(F32)
-            dm = (ect + mm(picks(down(recv[pl.ds(b, 1), :]), TILE), tile_grad)) * live(count, b)
+            dm = (ect + mm(picks(down(recv[:, rows]), TILE), tile_grad)) * live(count, b)
             scale_grad = scale_grad + jnp.sum(dm * hat, axis=0, keepdims=True)
             d = standard_back(dm * esc[...], hat, inv).astype(BF)
             dp = (mm_nt(d, es[...]) * silu_slope(pre)).astype(BF)
@@ -163,28 +180,30 @@
 
     scale_grad = jnp.zeros((1, L), F32)
     for t, tile_grad in enumerate(tiles):
-        scale_grad = lax.fori_loop(t * DEG, (t + 1) * DEG, block(tile_grad), scale_grad, unroll=2)
-    grads[384:512, :] = mm_tn(hid[...], du[...])
-    grads[256:384, :] = mm_tn(edges[...], dpre[...])
+        scale_grad = lax.fori_loop(t * DEG, (t + 1) * DEG, block(tile_grad), scale_grad, unroll=4)
+    grads[384:512, :] = mm_tn(hid[...], du[...]).astype(BF)
+    grads[256:384, :] = mm_tn(edges[...], dpre[...]).astype(BF)
     row = lax.broadcasted_iota(jnp.int32, (16, L), 0)
-    grads[896:912, :] = jnp.where(row == 0, scale_grad, jnp.where(row == 1, node_scale_grad, 0.0))
+    scales = jnp.where(row == 0, scale_grad, jnp.where(row == 1, node_scale_grad, 0.0))
+    grads[896:912, :] = scales.astype(BF)
     parts = []
     for t in range(p // TILE):
         total = jnp.zeros((TILE, L), F32)
         for j in range(DEG):
             b = t * DEG + j
-            total += mm(drops(recv[b:b + 1, :], 0, TILE), dpre[b * TILE:(b + 1) * TILE, :])
+            at = slice(b * TILE, (b + 1) * TILE)
+            total += mm(drops(recv[:, at], 0, TILE), dpre[at, :])
         parts.append(total.astype(BF))
     gr = jnp.concatenate(parts, axis=0)
-    grads[L:2 * L, :] = mm_tn(nb, gr)
+    grads[L:2 * L, :] = mm_tn(nb, gr).astype(BF)
     node_grad = node_grad + mm_nt(gr, wr)
-    ids = send_flat[...]
+    ids = table_ids(send[...], p, ghost_n // SLOTS)
     parts = [
         mm(drops(ids, k, L), dpre[...]).astype(BF) for k in range(0, p + ghost_n, L)
     ]
     gs = jnp.concatenate(parts[:p // L], axis=0)
     gg = jnp.concatenate(parts[p // L:], axis=0)
-    grads[:L, :] = mm_tn(nb, gs) + mm_tn(ghosts[...], gg)
+    grads[:L, :] = (mm_tn(nb, gs) + mm_tn(ghosts[...], gg)).astype(BF)
     ghost_grad[...] = mm_nt(gg, ws).astype(BF)
     return node_grad + mm_nt(gs, ws)
 
@@ -192,14 +211,17 @@
 def pick_ghosts(nodes, ghost_ids, picked):
     for c in range(SLOTS):
         picked[c * L:(c + 1) * L, :] = mm(
-            picks(down(ghost_ids[c:c + 1, :]), nodes.shape[0]), nodes[...]
+            picks(down(ghost_row(ghost_ids, c)), nodes.shape[0]), nodes[...]
         ).astype(BF)
 
 
-def put_back(ghost_flat, returned, p):
-    return jnp.concatenate(
-        [mm(drops(ghost_flat[...], k, L), returned[...]) for k in range(0, p, L)], axis=0
-    )
+def put_back(ghost_ids, returned, p):
+    ids = jnp.concatenate([ghost_row(ghost_ids, c) for c in range(SLOTS)], axis=1)
+    return jnp.concatenate([mm(drops(ids, k, L), returned[...]) for k in range(0, p, L)], axis=0)
+
+
+def layer_of(i, ef, es, esc, nf, ns, nsc):
+    return ef.at[i], es.at[i], esc.at[i:i + 1], nf.at[i], ns.at[i], nsc.at[i:i + 1]
 
 
 def pick_kernel(nodes, ghost_ids, picked):
@@ -208,28 +230,28 @@
 
 def first_kernel(count, nodes, ghosts, edges, send, recv, ghost_ids, ef, es, esc, nf, ns, nsc,
                  pre, edges_out, inb, nodes_out, picked, table, msg):
-    forward(nodes, ghosts, edges, send, recv, count[0], (ef, es, esc, nf, ns, nsc), table, msg,
+    forward(nodes, ghosts, edges, send, recv, count[0], layer_of(0, ef, es, esc, nf, ns, nsc), table, msg,
             pre, edges_out, inb, nodes_out)
     pick_ghosts(nodes_out, ghost_ids, picked)
 
 
-def last_kernel(count, nodes, ghosts, edges, send, send_flat, recv, node_ct, edge_ct, ef, es, esc,
+def last_kernel(count, nodes, ghosts, edges, send, recv, node_ct, edge_ct, ef, es, esc,
                 nf, ns, nsc, edges_out, nodes_out, edge_grad, ghost_grad, grads, node_grad,
                 table, msg, pre, inb, hid, du, dpre):
-    w = (ef, es, esc, nf, ns, nsc)
+    w = layer_of(1, ef, es, esc, nf, ns, nsc)
     forward(nodes, ghosts, edges, send, recv, count[0], w, table, msg, pre, edges_out, inb,
             nodes_out)
-    node_grad[...] = backward(nodes, ghosts, edges, send, send_flat, recv, count[0], w, pre, inb,
+    node_grad[...] = backward(nodes, ghosts, edges, send, recv, count[0], w, pre, inb,
                               node_ct[...].astype(F32), edge_ct, hid, du, dpre, edge_grad,
                               ghost_grad, grads)
 
 
-def low_kernel(count, nodes, ghosts, edges, send, send_flat, recv, ghost_flat, upper_grad,
+def low_kernel(count, nodes, ghosts, edges, send, recv, ghost_ids, upper_grad,
                returned, edge_ct, pre, inb, ef, es, esc, nf, ns, nsc,
                edge_grad, ghost_grad, grads, node_grad, hid, du, dpre):
-    w = (ef, es, esc, nf, ns, nsc)
-    ct = upper_grad[...] + put_back(ghost_flat, returned, nodes.shape[0])
-    node_grad[...] = backward(nodes, ghosts, edges, send, send_flat, recv, count[0], w, pre, inb,
+    w = layer_of(0, ef, es, esc, nf, ns, nsc)
+    ct = upper_grad[...] + put_back(ghost_ids, returned, nodes.shape[0])
+    node_grad[...] = backward(nodes, ghosts, edges, send, recv, count[0], w, pre, inb,
                               ct.astype(BF).astype(F32), edge_ct, hid, du, dpre, edge_grad,
                               ghost_grad, grads)
 
@@ -287,6 +309,106 @@
     finish_swap(found, copies, src, dst, send_sem, recv_sem)
 
 
+def reduce_kernel(gx, gy, rows, src, grads0, grads1, dst, total, packed, half, part, got_core,
+                  got_x, got_gx, send_sem, recv_sem):
+    x, y = lax.axis_index("gx"), lax.axis_index("gy")
+    core, chip = lax.rem(y, 2), y // 2
+    chips = gy // 2
+    found = neighbours(gx, gy)
+    keep = [rows // 2, rows // (2 * chips), rows // (2 * chips * gx)]
+    start = [0, core * keep[0], core * keep[0] + chip * keep[1]]
+    groups = [
+        (2, core, lambda j: (x, chip * 2 + j)),
+        (chips, chip, lambda j: (x, j * 2 + core)),
+        (gx, x, lambda j: (j, y)),
+    ]
+    barrier = pltpu.get_barrier_semaphore()
+    for there, place in found:
+        @pl.when(there)
+        def _():
+            pl.semaphore_signal(barrier, inc=1, device_id=place, device_id_type=MESH)
+    peers = sum(jnp.where(there, 1, 0) for there, _ in found)
+    for count, me, place in groups:
+        for d in range(1, count):
+            pl.semaphore_signal(barrier, inc=1, device_id=place(lax.rem(me + d, count)),
+                                device_id_type=MESH)
+            peers = peers + 1
+    for c, (there, _) in enumerate(found):
+        @pl.when(jnp.logical_not(there))
+        def _():
+            dst[c] = jnp.zeros(dst.shape[1:], dst.dtype)
+    n = grads0.shape[0]
+    packed[:n, :] = grads0[...]
+    packed[n:2 * n, :] = grads1[...]
+    packed[2 * n:, :] = jnp.zeros((rows - 2 * n, L), BF)
+    pl.semaphore_wait(barrier, peers)
+    swaps = swap(found, src, dst, send_sem, recv_sem)
+
+    def at(index, size):
+        return pl.ds(pl.multiple_of(index, 16), size)
+
+    sent = []
+    sem = SLOTS
+    held = packed
+    for (count, me, place), size, got, out in zip(
+        groups, keep, (got_core, got_x, got_gx), (half, part, total)
+    ):
+        copies = []
+        for d in range(1, count):
+            peer = lax.rem(me + d, count)
+            copies.append(pltpu.make_async_remote_copy(
+                src_ref=held.at[at(peer * size, size)], dst_ref=got.at[d - 1],
+                send_sem=send_sem.at[sem], recv_sem=recv_sem.at[sem],
+                device_id=place(peer), device_id_type=MESH,
+            ))
+            sem += 1
+            copies[-1].start()
+        mine = held[at(me * size, size), :].astype(F32)
+        for d, copy in enumerate(copies):
+            copy.wait_recv()
+            mine = mine + got[d].astype(F32)
+        if out is total:
+            out[at(start[2] + x * size, size), :] = mine.astype(BF)
+        else:
+            out[...] = mine.astype(BF)
+        sent += copies
+        held = out
+    for (count, me, place), size, first in reversed(list(zip(groups, keep, start))):
+        copies = []
+        own = total.at[at(first + me * size, size)]
+        for d in range(1, count):
+            copies.append(pltpu.make_async_remote_copy(
+                src_ref=own, dst_ref=own, send_sem=send_sem.at[sem], recv_sem=recv_sem.at[sem],
+                device_id=place(lax.rem(me + d, count)), device_id_type=MESH,
+            ))
+            copies[-1].start()
+            origin = lax.rem(me - d + count, count)
+            block = total.at[at(first + origin * size, size)]
+            copies.append(pltpu.make_async_remote_copy(
+                src_ref=block, dst_ref=block, send_sem=send_sem.at[sem], recv_sem=recv_sem.at[sem],
+                device_id=place(origin), device_id_type=MESH,
+            ))
+            sem += 1
+        for copy in copies[1::2]:
+            copy.wait_recv()
+        sent += copies[::2]
+    for copy in sent:
+        copy.wait_send()
+    finish_swap(found, swaps, src, dst, send_sem, recv_sem)
+
+
+def end_kernel(ghost_ids, lower, returned, total, node_grad, ef, es, esc, nf, ns, nsc):
+    p = lower.shape[0]
+    node_grad[...] = lower[...] + put_back(ghost_ids, returned, p)
+    for i in range(LAYERS):
+        base = i * 912
+        for out, first, last in ((ef, 0, 384), (es, 384, 512), (nf, 512, 768), (ns, 768, 896)):
+            out[i] = total[base + first:base + last, :].astype(F32)
+        scales = total[base + 896:base + 912, :].astype(F32)
+        esc[i:i + 1, :] = scales[:1, :]
+        nsc[i:i + 1, :] = scales[1:2, :]
+
+
 def solution(mesh):
     gx, gy = mesh.shape["gx"], mesh.shape["gy"]
 
@@ -318,36 +440,26 @@
                   node_first, node_second, node_scale):
         nodes, edges = latents[0, 0], edge_latents[0, 0]
         p, e = nodes.shape[0], edges.shape[0]
-        g = ghost_rows.shape[-1]
-        ghost_n = SLOTS * g
-        ids = senders[0, 0]
-        ids = jnp.where(ids >= p + 4 * g, ids - g, ids)
-        send, send_flat = ids.reshape(-1, TILE), ids.reshape(1, -1)
-        recv = receivers[0, 0].reshape(-1, TILE)
-        slots = ghost_rows[0, 0].reshape(9, g)
-        ghost_ids = jnp.concatenate([slots[:4], slots[5:]], axis=0)
-        ghost_flat = ghost_ids.reshape(1, -1)
+        ghost_n = SLOTS * ghost_rows.shape[-1]
+        send, recv = senders.reshape(1, e), receivers.reshape(1, e)
         count = edge_count.reshape(1)
-        weights = [
-            (edge_first[i], edge_second[i], edge_scale[i:i + 1], node_first[i], node_second[i],
-             node_scale[i:i + 1])
-            for i in range(LAYERS)
-        ]
+        weights = (edge_first, edge_second, edge_scale, node_first, node_second, node_scale)
 
         def s(shape, dtype):
             return jax.ShapeDtypeStruct(shape, dtype)
 
         back_scratch = [pltpu.VMEM((e, L), BF)] * 3
-        fore_scratch = [pltpu.VMEM((2 * p + ghost_n, L), BF), pltpu.VMEM((e, L), BF)]
-        grad_rows = s((912, L), F32)
-
-        picked = call(pick_kernel, s((ghost_n, L), BF), [], (nodes, ghost_ids), smem_first=False)
+        fore_scratch = [pltpu.VMEM((p + ghost_n + TILE + L, L), BF), pltpu.VMEM((e, L), BF)]
+        n = 912
+        grad_rows = s((n, L), BF)
+
+        picked = call(pick_kernel, s((ghost_n, L), BF), [], (nodes, ghost_rows), smem_first=False)
         ghosts0 = exchange(picked, 0)
         pre0, edges1, inb0, nodes1, picked1 = call(
             first_kernel,
             (s((e, L), F32), s((e, L), BF), s((p, L), BF), s((p, L), BF), s((ghost_n, L), BF)),
             fore_scratch,
-            (count, nodes, ghosts0, edges, send, recv, ghost_ids, *weights[0]),
+            (count, nodes, ghosts0, edges, send, recv, ghost_rows, *weights),
         )
         ghosts1 = exchange(picked1, 1)
         edges_out, nodes_out, edge_ct, ghost_ct, grads1, upper = call(
@@ -355,38 +467,48 @@
             (s((e, L), BF), s((p, L), BF), s((e, L), BF), s((ghost_n, L), BF), grad_rows,
              s((p, L), F32)),
             fore_scratch + [pltpu.VMEM((e, L), F32), pltpu.VMEM((p, L), BF)] + back_scratch,
-            (count, nodes1, ghosts1, edges1, send, send_flat, recv, node_cotangent[0, 0],
-             edge_cotangent[0, 0], *weights[1]),
-        )
-        total1 = lax.psum(grads1, ("gx", "gy"))
+            (count, nodes1, ghosts1, edges1, send, recv, node_cotangent[0, 0],
+             edge_cotangent[0, 0], *weights),
+        )
         returned1 = exchange(ghost_ct, 2)
         edge_grad, ghost_ct0, grads0, lower = call(
             low_kernel,
             (s((e, L), F32), s((ghost_n, L), BF), grad_rows, s((p, L), F32)),
             back_scratch,
-            (count, nodes, ghosts0, edges, send, send_flat, recv, ghost_flat, upper, returned1,
-             edge_ct, pre0, inb0, *weights[0]),
-        )
-        total0 = lax.psum(grads0, ("gx", "gy"))
-        returned0 = exchange(ghost_ct0, 3)
-
-        def end_kernel(ids_ref, lower_ref, returned_ref, out):
-            out[...] = lower_ref[...] + put_back(ids_ref, returned_ref, p)
-
-        node_grad = call(end_kernel, s((p, L), F32), [], (ghost_flat, lower, returned0),
-                         smem_first=False)
-        totals = jnp.stack([total0, total1])
+            (count, nodes, ghosts0, edges, send, recv, ghost_rows, upper, returned1,
+             edge_ct, pre0, inb0, *weights),
+        )
+        unit = 16 * gx * gy
+        rows = -(-2 * n // unit) * unit
+        chips = gy // 2
+        quarter = rows // (2 * chips)
+        sems = SLOTS + 2 * (1 + chips - 1 + gx - 1)
+        slots = (SLOTS, ghost_n // SLOTS, L)
+        returned0, total = call(
+            functools.partial(reduce_kernel, gx, gy, rows),
+            (s(slots, BF), s((rows, L), BF)),
+            [pltpu.VMEM((rows, L), BF), pltpu.VMEM((rows // 2, L), BF), pltpu.VMEM((quarter, L), BF),
+             pltpu.VMEM((1, rows // 2, L), BF), pltpu.VMEM((chips - 1, quarter, L), BF),
+             pltpu.VMEM((gx - 1, quarter // gx, L), BF),
+             pltpu.SemaphoreType.DMA((sems,)), pltpu.SemaphoreType.DMA((sems,))],
+            (ghost_ct0.reshape(slots), grads0, grads1),
+            smem_first=False,
+            collective_id=3,
+            has_side_effects=True,
+        )
+        node_grad, *weight_grads = call(
+            end_kernel,
+            (s((p, L), F32),) + tuple(s(w.shape, F32) for w in weights),
+            [],
+            (ghost_rows, lower, returned0.reshape(ghost_n, L), total),
+            smem_first=False,
+        )
         return (
             nodes_out[None, None],
             edges_out[None, None],
             node_grad[None, None],
             edge_grad[None, None],
-            totals[:, :384],
-            totals[:, 384:512],
-            totals[:, 896],
-            totals[:, 512:768],
-            totals[:, 768:896],
-            totals[:, 897],
+            *weight_grads,
         )
 
     cell = P("gx", "gy", None, None)

time: 238 us -> 111 us (0.47)
  waiting for transfers between devices: 121 us -> 0 us
  between operations: 14.9 us -> 1.51 us
  Pallas kernels: 84.8 us -> 97.4 us
  other arithmetic: 4.27 us -> 0 us
    psum x1 -> x0, waiting for transfers between devices: 121 us -> none  [on_device(): total0 = lax.psum(grads0, ('gx', 'gy'))]
    pallas_call x9, Pallas kernels: 84.8 us -> 97.4 us  [call(): pl.pallas_call(kernel, out_shape=shapes, in_specs=[SMEM if smem_first and...]
    unnamed x16 -> x43, local copies, waits for them, and re-layouts: 4.71 us -> 11.4 us
    slice x6 -> x0, local copies, waits for them, and re-layouts: 3.55 us -> none  [the longest x1 0.77 us: on_device(): totals[:, :384]]
    unnamed x3 -> x0, other arithmetic: 3.52 us -> none
    squeeze x4 -> x0, local copies, waits for them, and re-layouts: 2.67 us -> none  [the longest x1 0.96 us: on_device(): edge_first[i]]
  transfers between devices with their start and end apart: 1 -> 0, of which waited for: 1 -> 0; matrix products, arithmetic and copies ran while one was open for 0% -> 0% of each run, Pallas kernels for 3% -> 0%
where the time goes in v1:
time: 111 us; the launch traced here: 110 us
  Pallas kernels  97.4 us (88%)
  local copies, waits for them, and re-layouts  11.4 us (10%)
  between operations  1.51 us (1%)
    pallas_call x9, Pallas kernels, call(): pl.pallas_call(kernel, out_shape=shapes, in_specs=[SMEM if smem_first and...  97.4 us
    unnamed x43, local copies, waits for them, and re-layouts  11.4 us

profile of v1, /device:TPU:0, one launch (start us, length us, event | category | flops | bytes accessed | tf_op | source)
XLA Modules:
  0.0 110.3 jit_solution(8423742876953413842)
XLA Ops:
  0.6 0.0 copy-start.4
  1.3 0.7 copy.24.ghost_ids
  2.0 0.9 copy-done.5
  3.0 0.0 copy-start.19
  3.0 0.5 shard_map.213
  3.4 7.2 %shard_map.214 = bf16[8,128,128]{2,1,0:T(8,128)(2,1)S(1)} custom-call(bf16[8,128,128]{2,1,0:T(8,128)(2,1)S(1)} %bitcast.32), custom_call_target="tpu_custom_call" | custom-call | tf_op jit(solution)/shard_map/pallas_call | solution.py:416
  10.6 1.2 %copy-done = bf16[1,1,4096,128]{3,2,1,0:T(8,128)(2,1)S(1)} copy-done((bf16[1,1,4096,128]{3,2,1,0:T(8,128)(2,1)S(1)}, bf16[1,1,4096,128]{3,2,1,0:T(8,128)(2,1)}, u32[]{:S(2)}) %copy-start) | copy-done | bytes 1048600
  11.8 0.9 copy-done.3
  12.8 0.9 copy-done.6
  13.7 0.9 copy-done.8
  14.6 0.8 copy-done.11
  15.4 0.8 copy-done.13
  16.3 0.7 copy-done.15
  17.0 0.7 copy-done.16
  17.7 0.7 copy-done.18
  18.4 0.7 copy-done.20
  19.1 9.9 %shard_map.215 = (f32[4096,128]{1,0:T(8,128)S(1)}, bf16[4096,128]{1,0:T(8,128)(2,1)S(1)}, bf16[512,128]{1,0:T(8,128)(2,1)S(1)}, bf16[512,128]{1,0:T(8,128)(2,1)S(1)}, bf16[1024,128]{1,0:T(8,128)(2,1)S(1)}) custom-call(s32[1]{0:T(128)} %bitcast.19.count, bf16[512,128]{1,0:T(8,128)(2,1)S(1)} %bitcast.27, bf16[1024,128]{1,0:T(8,128)(2,1)S(1)} %bitcast.24, ...), custom_call_target="tpu_custom_call" | custom-call | tf_op jit(solution)/shard_map/pallas_call | solution.py:416
  28.9 1.3 %copy-done.2 = f32[4096,128]{1,0:T(8,128)} copy-done((f32[4096,128]{1,0:T(8,128)}, f32[4096,128]{1,0:T(8,128)S(1)}, u32[]{:S(2)}) %copy-start.2) | copy-done | bytes 2097176
  30.3 7.3 %shard_map.216 = bf16[8,128,128]{2,1,0:T(8,128)(2,1)S(1)} custom-call(bf16[8,128,128]{2,1,0:T(8,128)(2,1)S(1)} %bitcast.34), custom_call_target="tpu_custom_call" | custom-call | tf_op jit(solution)/shard_map/pallas_call | solution.py:416
  37.6 22.8 %shard_map.217 = (bf16[4096,128]{1,0:T(8,128)(2,1)}, bf16[512,128]{1,0:T(8,128)(2,1)}, bf16[4096,128]{1,0:T(8,128)(2,1)S(1)}, bf16[1024,128]{1,0:T(8,128)(2,1)S(...) custom-call(s32[1]{0:T(128)} %bitcast.20.count, bf16[512,128]{1,0:T(8,128)(2,1)S(1)} %get-tuple-element.34.nodes, ...), custom_call_target="tpu_custom_call" | custom-call | tf_op jit(solution)/shard_map/pallas_call | solution.py:416
  60.5 7.3 %shard_map.218 = bf16[8,128,128]{2,1,0:T(8,128)(2,1)S(1)} custom-call(bf16[8,128,128]{2,1,0:T(8,128)(2,1)S(1)} %bitcast.33), custom_call_target="tpu_custom_call" | custom-call | tf_op jit(solution)/shard_map/pallas_call | solution.py:416
  67.7 15.7 %shard_map.219 = (f32[4096,128]{1,0:T(8,128)}, bf16[1024,128]{1,0:T(8,128)(2,1)S(1)}, bf16[912,128]{1,0:T(8,128)(2,1)S(1)}, f32[512,128]{1,0:T(8,128)S(1)}) custom-call(s32[1]{0:T(128)} %bitcast.21.count, bf16[512,128]{1,0:T(8,128)(2,1)S(1)} %bitcast.28, bf16[1024,128]{1,0:T(8,128)(2,1)S(1)} %bitcast.25, bf16[4096,128]{1,0:T(8,128)(2,1)S(1)} %bitcast.23, ...), custom_call_target="tpu_custom_call" | custom-call | tf_op jit(solution)/shard_map/pallas_call | solution.py:416
  83.4 25.4 %shard_map.220 = (bf16[8,128,128]{2,1,0:T(8,128)(2,1)S(1)}, bf16[2048,128]{1,0:T(8,128)(2,1)S(1)}) custom-call(bf16[8,128,128]{2,1,0:T(8,128)(2,1)S(1)} %bitcast.35, bf16[912,128]{1,0:T(8,128)(2,1)S(1)} %get-tuple-element.46.grads0, bf16[912,128]{1,0:T(8,128)(2,1)S(1)} %get-tuple-element.47.grads1), custom_call_target="tpu_custom_call" | custom-call | tf_op jit(solution)/shard_map/pallas_call | solution.py:416
  108.9 1.4 %shard_map.221 = (f32[512,128]{1,0:T(8,128)}, f32[2,384,128]{2,1,0:T(8,128)}, f32[2,128,128]{2,1,0:T(8,128)}, f32[2,128]{1,0:T(2,128)}, f32[2,256,128]{2,1,0:T(8...) custom-call(s32[1,1,3,3,128]{4,3,2,1,0:T(4,128)S(1)} %copy.24.ghost_ids, f32[512,128]{1,0:T(8,128)S(1)} %get-tuple-element.44.lower, ...), custom_call_target="tpu_custom_call" | custom-call | tf_op jit(solution)/shard_map/pallas_call | solution.py:416
  (28 shorter events, 0.1 us)
Async XLA Ops:
  0.6 36.9 %copy-start.4 = (bf16[2,384,128]{2,1,0:T(8,128)(2,1)S(1)}, bf16[2,384,128]{2,1,0:T(8,128)(2,1)}, u32[]{:S(2)}) copy-start(bf16[2,384,128]{2,1,0:T(8,128)(2,1)} %ef.5) | copy-start | bytes 589828
  2.0 0.9 copy-start.5
  2.9 34.6 %copy-start.9 = (bf16[2,256,128]{2,1,0:T(8,128)(2,1)S(1)}, bf16[2,256,128]{2,1,0:T(8,128)(2,1)}, u32[]{:S(2)}) copy-start(bf16[2,256,128]{2,1,0:T(8,128)(2,1)} %nf.5) | copy-start | bytes 393220
  2.9 34.6 %copy-start.12 = (bf16[2,128,128]{2,1,0:T(8,128)(2,1)S(1)}, bf16[2,128,128]{2,1,0:T(8,128)(2,1)}, u32[]{:S(2)}) copy-start(bf16[2,128,128]{2,1,0:T(8,128)(2,1)} %es.5) | copy-start | bytes 196612
  2.9 34.6 %copy-start.14 = (bf16[2,128,128]{2,1,0:T(8,128)(2,1)S(1)}, bf16[2,128,128]{2,1,0:T(8,128)(2,1)}, u32[]{:S(2)}) copy-start(bf16[2,128,128]{2,1,0:T(8,128)(2,1)} %ns.5) | copy-start | bytes 196612
  2.9 34.6 %copy-start.17 = (bf16[1,1,512,128]{3,2,1,0:T(8,128)(2,1)S(1)}, bf16[1,1,512,128]{3,2,1,0:T(8,128)(2,1)}, u32[]{:S(2)}) copy-start(bf16[1,1,512,128]{3,2,1,0:T(8,128)(2,1)} %param.20) | copy-start | bytes 393220
  3.0 34.6 %copy-start.19 = (f32[2,128]{1,0:T(2,128)S(1)}, f32[2,128]{1,0:T(2,128)}, u32[]{:S(2)}) copy-start(f32[2,128]{1,0:T(2,128)} %esc.5) | copy-start | bytes 3076
  10.6 1.2 %copy-start = (bf16[1,1,4096,128]{3,2,1,0:T(8,128)(2,1)S(1)}, bf16[1,1,4096,128]{3,2,1,0:T(8,128)(2,1)}, u32[]{:S(2)}) copy-start(bf16[1,1,4096,128]{3,2,1,0:T(8,128)(2,1)} %param.15) | copy-start | bytes 3145732
  11.8 0.9 copy-start.3
  12.8 0.9 copy-start.6
  13.7 0.9 copy-start.8
  14.6 0.8 copy-start.11
  15.4 0.8 copy-start.13
  16.3 0.7 copy-start.15
  17.0 0.7 copy-start.16
  17.7 0.7 copy-start.18
  18.4 0.7 copy-start.20
  19.1 18.6 %copy-start.10 = (bf16[1,1,4096,128]{3,2,1,0:T(8,128)(2,1)S(1)}, bf16[1,1,4096,128]{3,2,1,0:T(8,128)(2,1)}, u32[]{:S(2)}) copy-start(bf16[1,1,4096,128]{3,2,1,0:T(8,128)(2,1)} %param.21) | copy-start | bytes 3145732
  28.9 1.3 %copy-start.2 = (f32[4096,128]{1,0:T(8,128)}, f32[4096,128]{1,0:T(8,128)S(1)}, u32[]{:S(2)}) copy-start(f32[4096,128]{1,0:T(8,128)S(1)} %get-tuple-element.42.pre) | copy-start | bytes 6291460
  30.3 37.5 %copy-start.1 = (bf16[1,1,4096,128]{3,2,1,0:T(8,128)(2,1)S(1)}, bf16[1,1,4096,128]{3,2,1,0:T(8,128)(2,1)}, u32[]{:S(2)}) copy-start(bf16[1,1,4096,128]{3,2,1,0:T(8,128)(2,1)} %param.15) | copy-start | bytes 3145732
  30.3 37.5 %copy-start.7 = (bf16[1,1,512,128]{3,2,1,0:T(8,128)(2,1)S(1)}, bf16[1,1,512,128]{3,2,1,0:T(8,128)(2,1)}, u32[]{:S(2)}) copy-start(bf16[1,1,512,128]{3,2,1,0:T(8,128)(2,1)} %param.14) | copy-start | bytes 393220

commit v2 on v1

--- a/solution.py
+++ b/solution.py
@@ -59,9 +59,9 @@
     return v / (1.0 + jnp.exp(-v))
 
 
-def silu_slope(v):
+def silu_parts(v):
     s = 1.0 / (1.0 + jnp.exp(-v))
-    return s * (1.0 + v * (1.0 - s))
+    return v * s, s * (1.0 + v * (1.0 - s))
 
 
 def standard(v):
@@ -95,11 +95,10 @@
     return ghost_ids[0, 0, a, b:b + 1, :]
 
 
-def forward(nodes, ghosts, edges, send, recv, count, w, table, msg, pre_out, edges_out,
+def forward(nodes, ghosts, edges, send_down, recv, recv_down, count, w, table, msg, pre_out, edges_out,
             inb_out, nodes_out):
     ef, es, esc, nf, ns, nsc = w
     p = nodes.shape[0]
-    g = ghosts.shape[0] // SLOTS
     size = p + ghosts.shape[0]
     ws, wr, we = (ef[i * L:(i + 1) * L, :] for i in range(3))
     table[:p, :] = mm(nodes[...], ws).astype(BF)
@@ -110,8 +109,8 @@
         rows = rows_of(b)
         left = jnp.concatenate(
             [
-                picks(down(table_ids(send[:, rows], p, g)), size),
-                picks(down(recv[:, rows]), TILE),
+                picks(send_down[rows, :], size),
+                picks(recv_down[rows, :], TILE),
                 edges[rows, :],
             ],
             axis=1,
@@ -139,7 +138,7 @@
     nodes_out[...] = (nodes[...].astype(F32) + hat * nsc[...]).astype(BF)
 
 
-def backward(nodes, ghosts, edges, send, recv, count, w, pre_in, inb, node_ct, edge_ct,
+def backward(nodes, ghosts, edges, send, recv, recv_down, count, w, pre_in, inb, node_ct, edge_ct,
              hid, du, dpre, edge_grad, ghost_grad, grads):
     ef, es, esc, nf, ns, nsc = w
     p = nodes.shape[0]
@@ -148,11 +147,12 @@
     ws, wr, we = (ef[i * L:(i + 1) * L, :] for i in range(3))
     nb = nodes[...]
     pre_n = mm(nb, nf[:L, :]) + mm(inb[...], nf[L:, :])
-    hid_n = silu(pre_n).astype(BF)
+    hid_n, slope_n = silu_parts(pre_n)
+    hid_n = hid_n.astype(BF)
     hat, inv = standard(mm(hid_n, ns[...]))
     node_scale_grad = jnp.sum(node_ct * hat, axis=0, keepdims=True)
     du_n = standard_back(node_ct * nsc[...], hat, inv).astype(BF)
-    dpre_n = (mm_nt(du_n, ns[...]).astype(BF).astype(F32) * silu_slope(pre_n)).astype(BF)
+    dpre_n = (mm_nt(du_n, ns[...]).astype(BF).astype(F32) * slope_n).astype(BF)
     grads[512:640, :] = mm_tn(nb, dpre_n).astype(BF)
     grads[640:768, :] = mm_tn(inb[...], dpre_n).astype(BF)
     grads[768:896, :] = mm_tn(hid_n, du_n).astype(BF)
@@ -164,13 +164,14 @@
         def body(b, scale_grad):
             rows = rows_of(b)
             pre = pre_in[rows, :]
-            h = silu(pre).astype(BF)
+            h, slope = silu_parts(pre)
+            h = h.astype(BF)
             hat, inv = standard(mm(h, es[...]))
             ect = edge_ct[rows, :].astype(F32)
-            dm = (ect + mm(picks(down(recv[:, rows]), TILE), tile_grad)) * live(count, b)
+            dm = (ect + mm(picks(recv_down[rows, :], TILE), tile_grad)) * live(count, b)
             scale_grad = scale_grad + jnp.sum(dm * hat, axis=0, keepdims=True)
             d = standard_back(dm * esc[...], hat, inv).astype(BF)
-            dp = (mm_nt(d, es[...]) * silu_slope(pre)).astype(BF)
+            dp = (mm_nt(d, es[...]) * slope).astype(BF)
             hid[rows, :] = h
             du[rows, :] = d
             dpre[rows, :] = dp
@@ -228,30 +229,30 @@
     pick_ghosts(nodes, ghost_ids, picked)
 
 
-def first_kernel(count, nodes, ghosts, edges, send, recv, ghost_ids, ef, es, esc, nf, ns, nsc,
+def first_kernel(count, nodes, ghosts, edges, send_down, recv, recv_down, ghost_ids, ef, es, esc, nf, ns, nsc,
                  pre, edges_out, inb, nodes_out, picked, table, msg):
-    forward(nodes, ghosts, edges, send, recv, count[0], layer_of(0, ef, es, esc, nf, ns, nsc), table, msg,
+    forward(nodes, ghosts, edges, send_down, recv, recv_down, count[0], layer_of(0, ef, es, esc, nf, ns, nsc), table, msg,
             pre, edges_out, inb, nodes_out)
     pick_ghosts(nodes_out, ghost_ids, picked)
 
 
-def last_kernel(count, nodes, ghosts, edges, send, recv, node_ct, edge_ct, ef, es, esc,
+def last_kernel(count, nodes, ghosts, edges, send, send_down, recv, recv_down, node_ct, edge_ct, ef, es, esc,
                 nf, ns, nsc, edges_out, nodes_out, edge_grad, ghost_grad, grads, node_grad,
                 table, msg, pre, inb, hid, du, dpre):
     w = layer_of(1, ef, es, esc, nf, ns, nsc)
-    forward(nodes, ghosts, edges, send, recv, count[0], w, table, msg, pre, edges_out, inb,
+    forward(nodes, ghosts, edges, send_down, recv, recv_down, count[0], w, table, msg, pre, edges_out, inb,
             nodes_out)
-    node_grad[...] = backward(nodes, ghosts, edges, send, recv, count[0], w, pre, inb,
+    node_grad[...] = backward(nodes, ghosts, edges, send, recv, recv_down, count[0], w, pre, inb,
                               node_ct[...].astype(F32), edge_ct, hid, du, dpre, edge_grad,
                               ghost_grad, grads)
 
 
-def low_kernel(count, nodes, ghosts, edges, send, recv, ghost_ids, upper_grad,
+def low_kernel(count, nodes, ghosts, edges, send, recv, recv_down, ghost_ids, upper_grad,
                returned, edge_ct, pre, inb, ef, es, esc, nf, ns, nsc,
                edge_grad, ghost_grad, grads, node_grad, hid, du, dpre):
     w = layer_of(0, ef, es, esc, nf, ns, nsc)
     ct = upper_grad[...] + put_back(ghost_ids, returned, nodes.shape[0])
-    node_grad[...] = backward(nodes, ghosts, edges, send, recv, count[0], w, pre, inb,
+    node_grad[...] = backward(nodes, ghosts, edges, send, recv, recv_down, count[0], w, pre, inb,
                               ct.astype(BF).astype(F32), edge_ct, hid, du, dpre, edge_grad,
                               ghost_grad, grads)
 
@@ -292,7 +293,17 @@
         pl.when(there)(arrival.wait_recv)
 
 
-def swap_kernel(gx, gy, src, dst, send_sem, recv_sem):
+def first_swap_kernel(gx, gy, p, src, send, recv, dst, send_down, recv_down, send_sem, recv_sem):
+    def columns():
+        ids = table_ids(send[...], p, src.shape[1])
+        for i in range(0, send.shape[1], TILE):
+            send_down[i:i + TILE, :] = down(ids[:, i:i + TILE])
+            recv_down[i:i + TILE, :] = down(recv[:, i:i + TILE])
+
+    swap_kernel(gx, gy, src, dst, send_sem, recv_sem, columns)
+
+
+def swap_kernel(gx, gy, src, dst, send_sem, recv_sem, beside=None):
     found = neighbours(gx, gy)
     barrier = pltpu.get_barrier_semaphore()
     for there, place in found:
@@ -306,6 +317,8 @@
     peers = sum(jnp.where(there, 1, 0) for there, _ in found)
     pl.semaphore_wait(barrier, peers)
     copies = swap(found, src, dst, send_sem, recv_sem)
+    if beside is not None:
+        beside()
     finish_swap(found, copies, src, dst, send_sem, recv_sem)
 
 
@@ -412,22 +425,29 @@
 def solution(mesh):
     gx, gy = mesh.shape["gx"], mesh.shape["gy"]
 
-    def call(kernel, shapes, scratch, args, smem_first=True, **params):
+    def call(kernel, mib, giga, shapes, scratch, args, smem_first=True, **params):
         return pl.pallas_call(
             kernel,
             out_shape=shapes,
             in_specs=[SMEM if smem_first and i == 0 else VMEM for i in range(len(args))],
             out_specs=jax.tree.map(lambda _: VMEM, shapes),
             scratch_shapes=scratch,
-            compiler_params=pltpu.CompilerParams(vmem_limit_bytes=48 * 2**20, **params),
+            cost_estimate=pl.CostEstimate(
+                flops=giga * 10**9, bytes_accessed=giga * 2**21, transcendentals=0
+            ),
+            compiler_params=pltpu.CompilerParams(vmem_limit_bytes=mib * 2**20, **params),
         )(*args)
+
+    swap_sems = [pltpu.SemaphoreType.DMA((SLOTS,)), pltpu.SemaphoreType.DMA((SLOTS,))]
 
     def exchange(value, collective_id):
         shape = (SLOTS, value.shape[0] // SLOTS, L)
         out = call(
             functools.partial(swap_kernel, gx, gy),
+            4,
+            7,
             jax.ShapeDtypeStruct(shape, BF),
-            [pltpu.SemaphoreType.DMA((SLOTS,)), pltpu.SemaphoreType.DMA((SLOTS,))],
+            swap_sems,
             (value.reshape(shape),),
             smem_first=False,
             collective_id=collective_id,
@@ -453,29 +473,47 @@
         n = 912
         grad_rows = s((n, L), BF)
 
-        picked = call(pick_kernel, s((ghost_n, L), BF), [], (nodes, ghost_rows), smem_first=False)
-        ghosts0 = exchange(picked, 0)
+        picked = call(pick_kernel, 8, 1, s((ghost_n, L), BF), [], (nodes, ghost_rows), smem_first=False)
+        slots = (SLOTS, ghost_n // SLOTS, L)
+        ghosts0, send_down, recv_down = call(
+            functools.partial(first_swap_kernel, gx, gy, p),
+            8,
+            7,
+            (s(slots, BF), s((e, L), I16), s((e, L), I16)),
+            swap_sems,
+            (picked.reshape(slots), send, recv),
+            smem_first=False,
+            collective_id=0,
+            has_side_effects=True,
+        )
+        ghosts0 = ghosts0.reshape(ghost_n, L)
         pre0, edges1, inb0, nodes1, picked1 = call(
             first_kernel,
+            24,
+            10,
             (s((e, L), F32), s((e, L), BF), s((p, L), BF), s((p, L), BF), s((ghost_n, L), BF)),
             fore_scratch,
-            (count, nodes, ghosts0, edges, send, recv, ghost_rows, *weights),
+            (count, nodes, ghosts0, edges, send_down, recv, recv_down, ghost_rows, *weights),
         )
         ghosts1 = exchange(picked1, 1)
         edges_out, nodes_out, edge_ct, ghost_ct, grads1, upper = call(
             last_kernel,
+            32,
+            22,
             (s((e, L), BF), s((p, L), BF), s((e, L), BF), s((ghost_n, L), BF), grad_rows,
              s((p, L), F32)),
             fore_scratch + [pltpu.VMEM((e, L), F32), pltpu.VMEM((p, L), BF)] + back_scratch,
-            (count, nodes1, ghosts1, edges1, send, recv, node_cotangent[0, 0],
+            (count, nodes1, ghosts1, edges1, send, send_down, recv, recv_down, node_cotangent[0, 0],
              edge_cotangent[0, 0], *weights),
         )
         returned1 = exchange(ghost_ct, 2)
         edge_grad, ghost_ct0, grads0, lower = call(
             low_kernel,
+            28,
+            15,
             (s((e, L), F32), s((ghost_n, L), BF), grad_rows, s((p, L), F32)),
             back_scratch,
-            (count, nodes, ghosts0, edges, send, recv, ghost_rows, upper, returned1,
+            (count, nodes, ghosts0, edges, send, recv, recv_down, ghost_rows, upper, returned1,
              edge_ct, pre0, inb0, *weights),
         )
         unit = 16 * gx * gy
@@ -483,9 +521,10 @@
         chips = gy // 2
         quarter = rows // (2 * chips)
         sems = SLOTS + 2 * (1 + chips - 1 + gx - 1)
-        slots = (SLOTS, ghost_n // SLOTS, L)
         returned0, total = call(
             functools.partial(reduce_kernel, gx, gy, rows),
+            12,
+            20,
             (s(slots, BF), s((rows, L), BF)),
             [pltpu.VMEM((rows, L), BF), pltpu.VMEM((rows // 2, L), BF), pltpu.VMEM((quarter, L), BF),
              pltpu.VMEM((1, rows // 2, L), BF), pltpu.VMEM((chips - 1, quarter, L), BF),
@@ -498,6 +537,8 @@
         )
         node_grad, *weight_grads = call(
             end_kernel,
+            12,
+            1,
             (s((p, L), F32),) + tuple(s(w.shape, F32) for w in weights),
             [],
             (ghost_rows, lower, returned0.reshape(ghost_n, L), total),

time: 111 us -> 101 us (0.910)
  local copies, waits for them, and re-layouts: 11.4 us -> 1.88 us
    unnamed x43 -> x27, local copies, waits for them, and re-layouts: 11.4 us -> 1.88 us
where the time goes in v2:
time: 101 us; the launch traced here: 100 us
  Pallas kernels  97 us (96%)
  local copies, waits for them, and re-layouts  1.88 us (2%)
  between operations  1.49 us (1%)
    pallas_call x9, Pallas kernels, call(): pl.pallas_call(kernel, out_shape=shapes, in_specs=[SMEM if smem_first and...  97 us

profile of v2, /device:TPU:0, one launch (start us, length us, event | category | flops | bytes accessed | tf_op | source)
XLA Modules:
  0.0 100.4 jit_solution(8728603813086195054)
XLA Ops:
  0.6 0.0 copy-start.9
  1.3 0.7 copy.24.ghost_ids
  2.0 0.9 copy-done.4
  2.9 0.5 shard_map.213
  3.4 0.0 copy-done.9
  3.4 0.2 copy-done.10
  3.6 0.0 copy-start.7
  3.7 0.0 copy-start.8
  3.7 0.0 copy-start.11
  3.7 0.0 copy-start.12
  3.7 7.2 %shard_map.214 = (bf16[8,128,128]{2,1,0:T(8,128)(2,1)S(1)}, s16[4096,128]{1,0:T(8,128)(2,1)S(1)}, s16[4096,128]{1,0:T(8,128)(2,1)S(1)}) custom-call(bf16[8,128,128]{2,1,0:T(8,128)(2,1)S(1)} %bitcast.44, s32[1,4096]{1,0:T(1,128)S(1)} %bitcast.29, s32[1,4096]{1,0:T(1,128)S(1)} %bitcast.32), custom_call_target="tpu_custom_call" | custom-call | flops 7000000000 | bytes 14680064 | tf_op jit(solution)/shard_map/pallas_call | solution.py:429
  10.9 0.0 copy-done.1
  10.9 0.0 copy-done.2
  10.9 9.6 %shard_map.215 = (f32[4096,128]{1,0:T(8,128)S(1)}, bf16[4096,128]{1,0:T(8,128)(2,1)S(1)}, bf16[512,128]{1,0:T(8,128)(2,1)S(1)}, bf16[512,128]{1,0:T(8,128)(2,1)S(1)}, bf16[1024,128]{1,0:T(8,128)(2,1)S(1)}) custom-call(s32[1]{0:T(128)} %bitcast.19.count, bf16[512,128]{1,0:T(8,128)(2,1)S(1)} %bitcast.27, bf16[1024,128]{1,0:T(8,128)(2,1)S(1)} %bitcast.36, ...), custom_call_target="tpu_custom_call" | custom-call | flops 10000000000 | bytes 20971520 | tf_op jit(solution)/shard_map/pallas_call | solution.py:429
  20.6 0.0 copy-start
  20.6 0.0 copy-start.3
  20.6 7.3 %shard_map.216 = bf16[8,128,128]{2,1,0:T(8,128)(2,1)S(1)} custom-call(bf16[8,128,128]{2,1,0:T(8,128)(2,1)S(1)} %bitcast.43), custom_call_target="tpu_custom_call" | custom-call | flops 7000000000 | bytes 14680064 | tf_op jit(solution)/shard_map/pallas_call | solution.py:429
  27.9 0.0 copy-done
  27.9 0.0 copy-done.3
  27.9 23.1 %shard_map.217 = (bf16[4096,128]{1,0:T(8,128)(2,1)}, bf16[512,128]{1,0:T(8,128)(2,1)}, bf16[4096,128]{1,0:T(8,128)(2,1)S(1)}, bf16[1024,128]{1,0:T(8,128)(2,1)S(...) custom-call(s32[1]{0:T(128)} %bitcast.20.count, bf16[512,128]{1,0:T(8,128)(2,1)S(1)} %get-tuple-element.40.nodes, ...), custom_call_target="tpu_custom_call" | custom-call | flops 22000001024 | bytes 46137344 | tf_op jit(solution)/shard_map/pallas_call | solution.py:429
  51.1 7.2 %shard_map.218 = bf16[8,128,128]{2,1,0:T(8,128)(2,1)S(1)} custom-call(bf16[8,128,128]{2,1,0:T(8,128)(2,1)S(1)} %bitcast.42), custom_call_target="tpu_custom_call" | custom-call | flops 7000000000 | bytes 14680064 | tf_op jit(solution)/shard_map/pallas_call | solution.py:429
  58.3 15.3 %shard_map.219 = (f32[4096,128]{1,0:T(8,128)}, bf16[1024,128]{1,0:T(8,128)(2,1)S(1)}, bf16[912,128]{1,0:T(8,128)(2,1)S(1)}, f32[512,128]{1,0:T(8,128)S(1)}) custom-call(s32[1]{0:T(128)} %bitcast.21.count, bf16[512,128]{1,0:T(8,128)(2,1)S(1)} %bitcast.28, bf16[1024,128]{1,0:T(8,128)(2,1)S(1)} %bitcast.37, bf16[4096,128]{1,0:T(8,128)(2,1)S(1)} %bitcast.24, ...), custom_call_target="tpu_custom_call" | custom-call | flops 15000000512 | bytes 31457280 | tf_op jit(solution)/shard_map/pallas_call | solution.py:429
  73.6 25.3 %shard_map.220 = (bf16[8,128,128]{2,1,0:T(8,128)(2,1)S(1)}, bf16[2048,128]{1,0:T(8,128)(2,1)S(1)}) custom-call(bf16[8,128,128]{2,1,0:T(8,128)(2,1)S(1)} %bitcast.38, bf16[912,128]{1,0:T(8,128)(2,1)S(1)} %get-tuple-element.52.grads0, bf16[912,128]{1,0:T(8,128)(2,1)S(1)} %get-tuple-element.53.grads1), custom_call_target="tpu_custom_call" | custom-call | flops 20000000000 | bytes 41943040 | tf_op jit(solution)/shard_map/pallas_call | solution.py:429
  99.0 1.4 %shard_map.221 = (f32[512,128]{1,0:T(8,128)}, f32[2,384,128]{2,1,0:T(8,128)}, f32[2,128,128]{2,1,0:T(8,128)}, f32[2,128]{1,0:T(2,128)}, f32[2,256,128]{2,1,0:T(8...) custom-call(s32[1,1,3,3,128]{4,3,2,1,0:T(4,128)S(1)} %copy.24.ghost_ids, f32[512,128]{1,0:T(8,128)S(1)} %get-tuple-element.50.lower, ...), custom_call_target="tpu_custom_call" | custom-call | flops 1000000000 | bytes 2097152 | tf_op jit(solution)/shard_map/pallas_call | solution.py:429
  (12 shorter events, 0.0 us)
Async XLA Ops:
  0.6 2.8 %copy-start.9 = (s32[1,1,4096]{2,1,0:T(1,128)S(1)}, s32[1,1,4096]{2,1,0:T(1,128)}, u32[]{:S(2)}) copy-start(s32[1,1,4096]{2,1,0:T(1,128)} %param.16) | copy-start | bytes 49156
  2.0 0.9 copy-start.4
  2.9 0.7 copy-start.10
  3.6 7.2 %copy-start.1 = (bf16[1,1,4096,128]{3,2,1,0:T(8,128)(2,1)S(1)}, bf16[1,1,4096,128]{3,2,1,0:T(8,128)(2,1)}, u32[]{:S(2)}) copy-start(bf16[1,1,4096,128]{3,2,1,0:T(8,128)(2,1)} %param.15) | copy-start | bytes 3145732
  3.6 7.2 %copy-start.2 = (bf16[2,384,128]{2,1,0:T(8,128)(2,1)S(1)}, bf16[2,384,128]{2,1,0:T(8,128)(2,1)}, u32[]{:S(2)}) copy-start(bf16[2,384,128]{2,1,0:T(8,128)(2,1)} %ef.5) | copy-start | bytes 589828
  3.6 7.2 %copy-start.5 = (bf16[1,1,512,128]{3,2,1,0:T(8,128)(2,1)S(1)}, bf16[1,1,512,128]{3,2,1,0:T(8,128)(2,1)}, u32[]{:S(2)}) copy-start(bf16[1,1,512,128]{3,2,1,0:T(8,128)(2,1)} %param.14) | copy-start | bytes 393220
  3.6 7.3 %copy-start.6 = (bf16[2,256,128]{2,1,0:T(8,128)(2,1)S(1)}, bf16[2,256,128]{2,1,0:T(8,128)(2,1)}, u32[]{:S(2)}) copy-start(bf16[2,256,128]{2,1,0:T(8,128)(2,1)} %nf.5) | copy-start | bytes 393220
  3.6 7.3 %copy-start.7 = (bf16[2,128,128]{2,1,0:T(8,128)(2,1)S(1)}, bf16[2,128,128]{2,1,0:T(8,128)(2,1)}, u32[]{:S(2)}) copy-start(bf16[2,128,128]{2,1,0:T(8,128)(2,1)} %es.5) | copy-start | bytes 196612
  3.7 7.3 %copy-start.8 = (bf16[2,128,128]{2,1,0:T(8,128)(2,1)S(1)}, bf16[2,128,128]{2,1,0:T(8,128)(2,1)}, u32[]{:S(2)}) copy-start(bf16[2,128,128]{2,1,0:T(8,128)(2,1)} %ns.5) | copy-start | bytes 196612
  3.7 7.3 %copy-start.11 = (f32[2,128]{1,0:T(2,128)S(1)}, f32[2,128]{1,0:T(2,128)}, u32[]{:S(2)}) copy-start(f32[2,128]{1,0:T(2,128)} %esc.5) | copy-start | bytes 3076
  3.7 7.3 %copy-start.12 = (f32[2,128]{1,0:T(2,128)S(1)}, f32[2,128]{1,0:T(2,128)}, u32[]{:S(2)}) copy-start(f32[2,128]{1,0:T(2,128)} %nsc.5) | copy-start | bytes 3076
  20.6 7.4 %copy-start = (bf16[1,1,4096,128]{3,2,1,0:T(8,128)(2,1)S(1)}, bf16[1,1,4096,128]{3,2,1,0:T(8,128)(2,1)}, u32[]{:S(2)}) copy-start(bf16[1,1,4096,128]{3,2,1,0:T(8,128)(2,1)} %param.21) | copy-start | bytes 3145732
  20.6 7.3 %copy-start.3 = (bf16[1,1,512,128]{3,2,1,0:T(8,128)(2,1)S(1)}, bf16[1,1,512,128]{3,2,1,0:T(8,128)(2,1)}, u32[]{:S(2)}) copy-start(bf16[1,1,512,128]{3,2,1,0:T(8,128)(2,1)} %param.20) | copy-start | bytes 393220

commit v3 on v2

--- a/solution.py
+++ b/solution.py
@@ -64,16 +64,22 @@
     return v * s, s * (1.0 + v * (1.0 - s))
 
 
+def lane_mean(v):
+    high = v.astype(BF)
+    low = (v - high.astype(F32)).astype(BF)
+    return mm(jnp.concatenate([high, low], axis=1), jnp.full((2 * L, L), 1.0 / L, BF))
+
+
 def standard(v):
-    center = jnp.mean(v, axis=-1, keepdims=True)
+    center = lane_mean(v)
     off = v - center
-    inv = lax.rsqrt(jnp.mean(off * off, axis=-1, keepdims=True) + EPS)
+    inv = lax.rsqrt(lane_mean(off * off) + EPS)
     return off * inv, inv
 
 
 def standard_back(g, hat, inv):
-    a = jnp.mean(g, axis=-1, keepdims=True)
-    b = jnp.mean(g * hat, axis=-1, keepdims=True)
+    a = lane_mean(g)
+    b = lane_mean(g * hat)
     return inv * (g - a - hat * b)
 
 

time: 101 us -> 114 us (1.13)
  Pallas kernels: 97 us -> 111 us
    pallas_call x9, Pallas kernels: 97 us -> 111 us  [call(): pl.pallas_call(kernel, out_shape=shapes, in_specs=[SMEM if smem_first and...]
where the time goes in v3:
time: 114 us
  Pallas kernels  111 us (97%)
  local copies, waits for them, and re-layouts  1.88 us (2%)
  between operations  1.49 us (1%)
    pallas_call x9, Pallas kernels, call(): pl.pallas_call(kernel, out_shape=shapes, in_specs=[SMEM if smem_first and...  111 us

profile of v3, /device:TPU:0, one launch (start us, length us, event | category | flops | bytes accessed | tf_op | source)
XLA Modules:
  0.0 114.0 jit_solution(5253686671748918198)
XLA Ops:
  1.3 0.7 copy.24.ghost_ids
  2.0 0.9 copy-done.4
  2.9 0.5 shard_map.213
  3.4 0.2 copy-done.10
  3.6 0.0 copy-start.7
  3.7 0.0 copy-start.8
  3.7 0.0 copy-start.11
  3.7 0.0 copy-start.12
  3.7 7.2 %shard_map.214 = (bf16[8,128,128]{2,1,0:T(8,128)(2,1)S(1)}, s16[4096,128]{1,0:T(8,128)(2,1)S(1)}, s16[4096,128]{1,0:T(8,128)(2,1)S(1)}) custom-call(bf16[8,128,128]{2,1,0:T(8,128)(2,1)S(1)} %bitcast.44, s32[1,4096]{1,0:T(1,128)S(1)} %bitcast.29, s32[1,4096]{1,0:T(1,128)S(1)} %bitcast.32), custom_call_target="tpu_custom_call" | custom-call | flops 7000000000 | bytes 14680064 | tf_op jit(solution)/shard_map/pallas_call | solution.py:435
  10.9 0.0 copy-done.1
  10.9 0.0 copy-done.2
  10.9 0.0 copy-done.5
  10.9 0.0 copy-done.6
  10.9 0.0 copy-done.7
  10.9 0.0 copy-done.8
  10.9 13.5 %shard_map.215 = (f32[4096,128]{1,0:T(8,128)S(1)}, bf16[4096,128]{1,0:T(8,128)(2,1)S(1)}, bf16[512,128]{1,0:T(8,128)(2,1)S(1)}, bf16[512,128]{1,0:T(8,128)(2,1)S(1)}, bf16[1024,128]{1,0:T(8,128)(2,1)S(1)}) custom-call(s32[1]{0:T(128)} %bitcast.19.count, bf16[512,128]{1,0:T(8,128)(2,1)S(1)} %bitcast.27, bf16[1024,128]{1,0:T(8,128)(2,1)S(1)} %bitcast.36, ...), custom_call_target="tpu_custom_call" | custom-call | flops 10000000000 | bytes 20971520 | tf_op jit(solution)/shard_map/pallas_call | solution.py:435
  24.5 0.0 copy-start
  24.5 0.0 copy-start.3
  24.5 7.3 %shard_map.216 = bf16[8,128,128]{2,1,0:T(8,128)(2,1)S(1)} custom-call(bf16[8,128,128]{2,1,0:T(8,128)(2,1)S(1)} %bitcast.43), custom_call_target="tpu_custom_call" | custom-call | flops 7000000000 | bytes 14680064 | tf_op jit(solution)/shard_map/pallas_call | solution.py:435
  31.8 30.0 %shard_map.217 = (bf16[4096,128]{1,0:T(8,128)(2,1)}, bf16[512,128]{1,0:T(8,128)(2,1)}, bf16[4096,128]{1,0:T(8,128)(2,1)S(1)}, bf16[1024,128]{1,0:T(8,128)(2,1)S(...) custom-call(s32[1]{0:T(128)} %bitcast.20.count, bf16[512,128]{1,0:T(8,128)(2,1)S(1)} %get-tuple-element.40.nodes, ...), custom_call_target="tpu_custom_call" | custom-call | flops 22000001024 | bytes 46137344 | tf_op jit(solution)/shard_map/pallas_call | solution.py:435
  61.8 7.2 %shard_map.218 = bf16[8,128,128]{2,1,0:T(8,128)(2,1)S(1)} custom-call(bf16[8,128,128]{2,1,0:T(8,128)(2,1)S(1)} %bitcast.42), custom_call_target="tpu_custom_call" | custom-call | flops 7000000000 | bytes 14680064 | tf_op jit(solution)/shard_map/pallas_call | solution.py:435
  69.1 18.1 %shard_map.219 = (f32[4096,128]{1,0:T(8,128)}, bf16[1024,128]{1,0:T(8,128)(2,1)S(1)}, bf16[912,128]{1,0:T(8,128)(2,1)S(1)}, f32[512,128]{1,0:T(8,128)S(1)}) custom-call(s32[1]{0:T(128)} %bitcast.21.count, bf16[512,128]{1,0:T(8,128)(2,1)S(1)} %bitcast.28, bf16[1024,128]{1,0:T(8,128)(2,1)S(1)} %bitcast.37, bf16[4096,128]{1,0:T(8,128)(2,1)S(1)} %bitcast.24, ...), custom_call_target="tpu_custom_call" | custom-call | flops 15000000512 | bytes 31457280 | tf_op jit(solution)/shard_map/pallas_call | solution.py:435
  87.2 25.3 %shard_map.220 = (bf16[8,128,128]{2,1,0:T(8,128)(2,1)S(1)}, bf16[2048,128]{1,0:T(8,128)(2,1)S(1)}) custom-call(bf16[8,128,128]{2,1,0:T(8,128)(2,1)S(1)} %bitcast.38, bf16[912,128]{1,0:T(8,128)(2,1)S(1)} %get-tuple-element.52.grads0, bf16[912,128]{1,0:T(8,128)(2,1)S(1)} %get-tuple-element.53.grads1), custom_call_target="tpu_custom_call" | custom-call | flops 20000000000 | bytes 41943040 | tf_op jit(solution)/shard_map/pallas_call | solution.py:435
  112.6 1.4 %shard_map.221 = (f32[512,128]{1,0:T(8,128)}, f32[2,384,128]{2,1,0:T(8,128)}, f32[2,128,128]{2,1,0:T(8,128)}, f32[2,128]{1,0:T(2,128)}, f32[2,256,128]{2,1,0:T(8...) custom-call(s32[1,1,3,3,128]{4,3,2,1,0:T(4,128)S(1)} %copy.24.ghost_ids, f32[512,128]{1,0:T(8,128)S(1)} %get-tuple-element.50.lower, ...), custom_call_target="tpu_custom_call" | custom-call | flops 1000000000 | bytes 2097152 | tf_op jit(solution)/shard_map/pallas_call | solution.py:435
  (12 shorter events, 0.0 us)
Async XLA Ops:
  0.6 2.8 %copy-start.9 = (s32[1,1,4096]{2,1,0:T(1,128)S(1)}, s32[1,1,4096]{2,1,0:T(1,128)}, u32[]{:S(2)}) copy-start(s32[1,1,4096]{2,1,0:T(1,128)} %param.16) | copy-start | bytes 49156
  2.0 0.9 copy-start.4
  2.9 0.7 copy-start.10
  3.6 7.2 %copy-start.1 = (bf16[1,1,4096,128]{3,2,1,0:T(8,128)(2,1)S(1)}, bf16[1,1,4096,128]{3,2,1,0:T(8,128)(2,1)}, u32[]{:S(2)}) copy-start(bf16[1,1,4096,128]{3,2,1,0:T(8,128)(2,1)} %param.15) | copy-start | bytes 3145732
  3.6 7.2 %copy-start.2 = (bf16[2,384,128]{2,1,0:T(8,128)(2,1)S(1)}, bf16[2,384,128]{2,1,0:T(8,128)(2,1)}, u32[]{:S(2)}) copy-start(bf16[2,384,128]{2,1,0:T(8,128)(2,1)} %ef.5) | copy-start | bytes 589828
  3.6 7.2 %copy-start.5 = (bf16[1,1,512,128]{3,2,1,0:T(8,128)(2,1)S(1)}, bf16[1,1,512,128]{3,2,1,0:T(8,128)(2,1)}, u32[]{:S(2)}) copy-start(bf16[1,1,512,128]{3,2,1,0:T(8,128)(2,1)} %param.14) | copy-start | bytes 393220
  3.6 7.3 %copy-start.6 = (bf16[2,256,128]{2,1,0:T(8,128)(2,1)S(1)}, bf16[2,256,128]{2,1,0:T(8,128)(2,1)}, u32[]{:S(2)}) copy-start(bf16[2,256,128]{2,1,0:T(8,128)(2,1)} %nf.5) | copy-start | bytes 393220
  3.6 7.3 %copy-start.7 = (bf16[2,128,128]{2,1,0:T(8,128)(2,1)S(1)}, bf16[2,128,128]{2,1,0:T(8,128)(2,1)}, u32[]{:S(2)}) copy-start(bf16[2,128,128]{2,1,0:T(8,128)(2,1)} %es.5) | copy-start | bytes 196612
  3.7 7.3 %copy-start.8 = (bf16[2,128,128]{2,1,0:T(8,128)(2,1)S(1)}, bf16[2,128,128]{2,1,0:T(8,128)(2,1)}, u32[]{:S(2)}) copy-start(bf16[2,128,128]{2,1,0:T(8,128)(2,1)} %ns.5) | copy-start | bytes 196612
  3.7 7.3 %copy-start.11 = (f32[2,128]{1,0:T(2,128)S(1)}, f32[2,128]{1,0:T(2,128)}, u32[]{:S(2)}) copy-start(f32[2,128]{1,0:T(2,128)} %esc.5) | copy-start | bytes 3076
  3.7 7.3 %copy-start.12 = (f32[2,128]{1,0:T(2,128)S(1)}, f32[2,128]{1,0:T(2,128)}, u32[]{:S(2)}) copy-start(f32[2,128]{1,0:T(2,128)} %nsc.5) | copy-start | bytes 3076
  24.5 7.4 %copy-start = (bf16[1,1,4096,128]{3,2,1,0:T(8,128)(2,1)S(1)}, bf16[1,1,4096,128]{3,2,1,0:T(8,128)(2,1)}, u32[]{:S(2)}) copy-start(bf16[1,1,4096,128]{3,2,1,0:T(8,128)(2,1)} %param.21) | copy-start | bytes 3145732
  24.5 7.3 %copy-start.3 = (bf16[1,1,512,128]{3,2,1,0:T(8,128)(2,1)S(1)}, bf16[1,1,512,128]{3,2,1,0:T(8,128)(2,1)}, u32[]{:S(2)}) copy-start(bf16[1,1,512,128]{3,2,1,0:T(8,128)(2,1)} %param.20) | copy-start | bytes 393220
